TPU v7x, 1024 devices: a whole 4x8x16 slice. The times are simulated.
1024 devices in a mesh: row: 64 (over y, z_lo), col: 16 (over x, z_hi, core).
Axes of the slice: x: 4, y: 8, z: 16 (z_hi: 2, z_lo: 8; z = z_hi * 8 + z_lo), core: 2. Of those that a mesh axis runs over, the one named last changes fastest.
Arguments:
- vectors: bfloat16 [4096, 4, 256], P(('row', 'col')), may hold values from -6 to 6
- tiles: bfloat16 [64, 16, 6, 256, 256], P('row', 'col'), may hold values from -0.375 to 0.375
- tile_rows: int32 [64, 16, 6], P('row', 'col'), may hold values from 0 to 63, as said below
- tile_cols: int32 [64, 16, 6], P('row', 'col'), may hold values from 0 to 255
- tile_counts: int32 [64, 16], P('row', 'col'), may hold values from 1 to 6, as said below
Outputs:
- product: float32 [4096, 4, 256], P(('row', 'col'))
Inputs may be any that keep to these rules, and one draw needn't show every extreme that they name: The first tile_counts slots of a grid position hold its live tiles. `tile_rows`: for every slot the global row block is not after the global column block.
All inputs are finite; a program needn't handle non-finite values.
Results may differ from a plain program's by a relative error of at most 0.00065.
Values may be sent and summed in bfloat16 or wider, within the bound.
A program may use at most 32 MiB of HBM per device.

v0:
```python
import jax
import jax.numpy as jnp
from jax import lax
from jax.sharding import PartitionSpec as P


def place_blocks(contributions, targets, block_span):
    onehot = (targets[:, None] == jnp.arange(block_span, dtype=jnp.int32)[None, :]).astype(
        jnp.float32
    )
    return jnp.einsum("sb,svd->bvd", onehot, contributions, precision=lax.Precision.HIGHEST)


def on_device(vectors, tiles, tile_rows, tile_cols, tile_counts):
    piece_blocks = vectors.shape[0]
    blocks = tiles[0, 0]
    row_index = tile_rows[0, 0]
    column_index = tile_cols[0, 0]
    slot_order = jnp.arange(blocks.shape[0], dtype=jnp.int32)
    live_mask = (slot_order < tile_counts[0, 0]).astype(jnp.float32)[:, None, None]
    segment = lax.all_gather(vectors, "row", axis=0, tiled=True)
    slab = lax.all_gather(vectors, "col", axis=0, tiled=True)
    column_vectors = jnp.take(segment, column_index, axis=0)
    row_vectors = jnp.take(slab, row_index, axis=0)
    to_rows = (
        lax.dot_general(
            column_vectors, blocks, (((2,), (2,)), ((0,), (0,))), preferred_element_type=jnp.float32
        )
        * live_mask
    )
    to_columns = (
        lax.dot_general(
            row_vectors, blocks, (((2,), (1,)), ((0,), (0,))), preferred_element_type=jnp.float32
        )
        * live_mask
    )
    own_rows = lax.psum_scatter(
        place_blocks(to_rows, row_index, piece_blocks * lax.axis_size("col")),
        "col",
        scatter_dimension=0,
        tiled=True,
    )
    own_columns = lax.psum_scatter(
        place_blocks(to_columns, column_index, piece_blocks * lax.axis_size("row")),
        "row",
        scatter_dimension=0,
        tiled=True,
    )
    return own_rows + own_columns


def solution(mesh):
    placed = (
        P(("row", "col"), None, None),
        P("row", "col", None, None, None),
        P("row", "col", None),
        P("row", "col", None),
        P("row", "col"),
    )
    return jax.shard_map(
        on_device,
        mesh=mesh,
        in_specs=placed,
        out_specs=P(("row", "col"), None, None),
        check_vma=False,
    )
```

profile of v0, /device:TPU:2, one launch (start us, length us, event | category | flops | bytes accessed | tf_op | source)
XLA Modules:
  0.0 1416.6 jit_solution(9827878498549065699)
XLA Ops:
  6.5 0.0 copy-start
  6.5 0.0 copy-start.2
  6.5 0.0 copy-start.1
  6.5 0.0 all-reduce.5.cloned.1.call-start
  6.5 0.7 fusion.20
  7.3 0.0 copy-done.2
  8.0 0.0 copy-done.1
  8.0 243.7 %all_gather.6 = bf16[256,4,256]{2,1,0:T(4,128)(2,1)S(1)} all-gather(bf16[4,4,256]{2,1,0:T(4,128)(2,1)S(1)} %copy-done.1), channel_id=1, replica_groups=mesh['row'=64,'col'=16] {'row'}, dimensions={0}, use_global_device_ids=true | all-gather | bytes 532480 | tf_op jit(solution)/shard_map/all_gather | solution.py:21
  251.6 0.6 gather_fusion
  252.2 0.0 copy-done
  252.2 0.3 fusion.2
  252.5 0.0 copy-start.3
  252.5 0.7 copy-done.3
  253.2 1.1 fusion.5
  254.3 0.0 all-reduce.5.cloned.1.call-update
  254.3 0.0 all-reduce.7.cloned.1.call-start
  254.4 43.7 %all_gather.7 = bf16[64,4,256]{2,1,0:T(4,128)(2,1)S(1)} all-gather(bf16[4,4,256]{2,1,0:T(4,128)(2,1)S(1)} %copy-done.1), channel_id=1, replica_groups=mesh['row'=64,'col'=16] {'col'}, dimensions={0}, use_global_device_ids=true | all-gather | bytes 139264 | tf_op jit(solution)/shard_map/all_gather | solution.py:22
  298.1 0.6 gather_fusion.1
  298.7 0.2 fusion
  298.9 1.7 fusion.4
  300.6 0.0 all-reduce.7.cloned.1.call-update
  300.7 1.4 dynamic-slice
  302.0 1.3 dynamic-slice.2
  304.6 199.5 %all-reduce.5.cloned.1.call-done = f32[64,4,256]{2,0,1:T(8,128)} async-done(((f32[64,4,256]{2,0,1:T(8,128)}), f32[64,4,256]{2,0,1:T(8,128)}) %all-reduce.5.cloned.1.call-update) | async-done | bytes 262160
  504.2 904.2 %all-reduce.7.cloned.1.call-done = f32[256,4,256]{2,0,1:T(8,128)} async-done(((f32[256,4,256]{2,0,1:T(8,128)}), f32[256,4,256]{2,0,1:T(8,128)}) %all-reduce.7.cloned.1.call-update) | async-done | bytes 1048592
  1408.4 0.8 dynamic-slice_add_fusion
  1409.2 0.6 copy.7
  (6 shorter events, 0.0 us)
Async XLA Ops:
  6.5 245.7 %copy-start = (bf16[1,1,6,256,256]{4,3,2,1,0:T(8,128)(2,1)S(1)}, bf16[1,1,6,256,256]{4,3,2,1,0:T(8,128)(2,1)}, u32[]{:S(2)}) copy-start(bf16[1,1,6,256,256]{4,3,2,1,0:T(8,128)(2,1)} %param.6) | copy-start | bytes 2359300
  6.5 0.7 copy-start.2
  6.5 1.4 copy-start.1
  6.5 497.6 %all-reduce.5.cloned.1.call-start = ((), (), s32[]{:S(2)}) async-start(), calls=%async_computation | async-start | bytes 524288
  252.5 0.7 copy-start.3
  254.3 1154.1 %all-reduce.7.cloned.1.call-start = ((), (), s32[]{:S(2)}) async-start(), calls=%async_computation.1 | async-start | bytes 2097152
Sparse Core Ops, SparseCore 0:
  254.4 249.6 all-reduce.4
  508.1 900.2 all-reduce.6
where the time goes:
time: 1420 us
  waiting for transfers between devices  1100 us (77%)
  blocking collectives  287 us (20%)
  between operations  15.4 us (1%)
    unnamed x4, waiting for transfers between devices  1100 us
    all_gather x1, blocking collectives, on_device(): segment = lax.all_gather(vectors, 'row', axis=0, tiled=True)  244 us
    all_gather x1, blocking collectives, on_device(): slab = lax.all_gather(vectors, 'col', axis=0, tiled=True)  43.7 us
  transfers between devices with their start and end apart: 2, of which 2 were waited for; matrix products, arithmetic and copies ran while one was open for 0% of the time, Pallas kernels for 0%

commit v1 on v0

v1 whole, which is shorter than its diff:
```python
import functools

import jax
import jax.numpy as jnp
from jax import lax
from jax.experimental import pallas as pl
from jax.experimental.pallas import tpu as pltpu
from jax.sharding import PartitionSpec as P

MESH = pl.DeviceIdType.MESH
NVEC = 4
TILE = 256
VB = 4
ROWS = VB * NVEC
PAD = 8
SLOT_ROWS = PAD * NVEC
LANES = 128
NONE = -(2**20)

H_VEC, G_CODE, Y_CODE, Z_VEC, G_VEC, Y_VEC, Y_PROD, G_PROD, Z_PROD, H_PROD = range(10)


def widen(row_of):
    sub = lax.broadcasted_iota(jnp.int32, (8, LANES), 0)
    pieces = []
    for k in range(PAD // 2):
        low = jnp.broadcast_to(row_of(2 * k), (8, LANES))
        high = jnp.broadcast_to(row_of(2 * k + 1), (8, LANES))
        pieces.append(jnp.where(sub < 4, low, high) + (sub & 3))
    return jnp.concatenate(pieces, axis=0)


def onehot(codes, base):
    lane = lax.broadcasted_iota(jnp.int32, codes.shape, 1)
    return jnp.where(codes == lane + base, 1.0, 0.0).astype(jnp.float32)


def place(matrix, products):
    high = products.astype(jnp.bfloat16)
    low = (products - high.astype(jnp.float32)).astype(jnp.bfloat16)
    return jnp.dot(matrix, high, preferred_element_type=jnp.float32) + jnp.dot(
        matrix, low, preferred_element_type=jnp.float32
    )


def kernel(
    sizes,
    vec_hbm, tiles_hbm, rows_hbm, cols_hbm, counts_hbm,
    out_ref,
    vin, tiles, rows_s, cols_s, counts_s,
    vz, vh, vg, ccode, rcode, ysend, yrecv, cprod, rprod, zsend, zrecv, hsend, hrecv,
    local_sem, send_sem, recv_sem,
):
    ny, nz, nx, nh, nc = sizes
    ng = nx * nc
    slots = tiles.shape[0]
    live_rows = slots * NVEC
    row, col = lax.axis_index("row"), lax.axis_index("col")
    y, z = row // nz, row % nz
    x, h, c = col // (nh * nc), (col // nc) % nh, col % nc
    g = x * nc + c

    def at(y_, z_, x_, h_, c_):
        return (y_ * nz + z_, (x_ * nh + h_) * nc + c_)

    def y_peer(k):
        p = lax.rem(y + k, ny)
        return p, at(p, z, x, h, c)

    def z_peer(k):
        p = lax.rem(z + k, nz)
        return p, at(y, p, x, h, c)

    def g_peer(k):
        p = lax.rem(g + k, ng)
        return p, at(y, z, p // nc, h, lax.rem(p, nc))

    h_other = nh - 1 - h
    h_id = at(y, z, x, h_other, c)
    groups = ((y_peer, ny), (z_peer, nz), (g_peer, ng))

    barrier = pltpu.get_barrier_semaphore()
    for peer, n in groups:
        @pl.loop(1, n)
        def _(k, peer=peer):
            pl.semaphore_signal(barrier, inc=1, device_id=peer(k)[1], device_id_type=MESH)
    pl.semaphore_signal(barrier, inc=1, device_id=h_id, device_id_type=MESH)

    locals_ = [
        pltpu.make_async_copy(src, dst, local_sem.at[i])
        for i, (src, dst) in enumerate(
            (
                (vec_hbm, vin),
                (rows_hbm, rows_s),
                (cols_hbm, cols_s),
                (counts_hbm, counts_s),
                (tiles_hbm.at[0, 0], tiles),
            )
        )
    ]
    for copy in locals_:
        copy.start()

    def send(which, src, dst, device_id):
        pltpu.make_async_remote_copy(
            src_ref=src,
            dst_ref=dst,
            send_sem=send_sem.at[which],
            recv_sem=recv_sem.at[which],
            device_id=device_id,
            device_id_type=MESH,
        ).start()

    def wait(sem, ref):
        pltpu.make_async_copy(ref, ref, sem).wait()

    def send_all(which, peer, n, src_of, dst):
        @pl.loop(1, n)
        def _(k):
            p, device_id = peer(k)
            send(which, src_of(p), dst, device_id)

    tail = SLOT_ROWS - live_rows
    if tail:
        cprod[:, live_rows:, :] = jnp.zeros((ny, tail, TILE), jnp.float32)
        rprod[:, live_rows:, :] = jnp.zeros((ng, tail, TILE), jnp.float32)

    locals_[0].wait()
    own = jnp.concatenate([vin[j].astype(jnp.float32) for j in range(VB)], axis=0)
    own = own.astype(jnp.bfloat16)
    vz[z] = own
    vh[h] = own
    for i in (1, 2, 3):
        locals_[i].wait()
    live = counts_s[0, 0]
    sub = lax.broadcasted_iota(jnp.int32, (PAD, LANES), 0)
    col_codes = jnp.full((PAD, LANES), NONE, jnp.int32)
    row_codes = col_codes
    for s in range(slots):
        q = cols_s[0, 0, s]
        p = rows_s[0, 0, s]
        owner, block = p // VB, p % VB
        px, ph, pc = owner // (nh * nc), (owner // nc) % nh, owner % nc
        place_at = ((px * nc + pc) * nh + ph) * ROWS + block * NVEC
        col_codes = jnp.where(sub == s, jnp.where(s < live, q * NVEC, NONE), col_codes)
        row_codes = jnp.where(sub == s, jnp.where(s < live, place_at, NONE), row_codes)
    ccode[y] = col_codes
    rcode[g] = row_codes

    pl.semaphore_wait(barrier, ny + nz + ng - 3 + 1)

    send(H_VEC, vh.at[h], vh.at[h], h_id)
    send_all(G_CODE, g_peer, ng, lambda p: rcode.at[g], rcode.at[g])
    send_all(Y_CODE, y_peer, ny, lambda p: ccode.at[y], ccode.at[y])
    send_all(Z_VEC, z_peer, nz, lambda p: vz.at[z], vz.at[z])

    wait(recv_sem.at[H_VEC], hsend_like(vh))
    vg[g] = vh[...].reshape(nh * ROWS, TILE)
    send_all(G_VEC, g_peer, ng, lambda p: vg.at[g], vg.at[g])

    wait(recv_sem.at[Y_CODE], ccode.at[pl.ds(0, ny - 1)])
    col_sel = jnp.concatenate(
        [
            onehot(widen(lambda s, p=p: ccode[p, s : s + 1, :]), y * (nz * ROWS))
            for p in range(ny)
        ],
        axis=0,
    )
    wait(recv_sem.at[Z_VEC], vz.at[pl.ds(0, nz - 1)])
    plane = vz[...].reshape(nz * ROWS, TILE)
    picked = jnp.dot(
        col_sel[:, : nz * ROWS].astype(jnp.bfloat16), plane, preferred_element_type=jnp.float32
    )
    ysend[...] = picked.astype(jnp.bfloat16).reshape(ny, SLOT_ROWS, TILE)
    send_all(Y_VEC, y_peer, ny, lambda p: ysend.at[p], yrecv.at[y])
    yrecv[y] = ysend[y]

    own_row_codes = widen(lambda s: row_codes[s : s + 1, :])
    slab_rows = ng * nh * ROWS
    pieces = [
        onehot(own_row_codes, b)[:, : min(LANES, slab_rows - b)]
        for b in range(0, slab_rows, LANES)
    ]
    row_sel = jnp.concatenate(pieces, axis=1).astype(jnp.bfloat16)
    half = lax.broadcasted_iota(jnp.int32, (8, TILE), 0) < 4

    def apply(vectors, contract):
        outs = []
        for k in range((slots + 1) // 2):
            pair = vectors[8 * k : 8 * k + 8].astype(jnp.bfloat16)
            both = [
                lax.dot_general(
                    pair,
                    tiles[min(2 * k + i, slots - 1)],
                    (((1,), (contract,)), ((), ())),
                    preferred_element_type=jnp.float32,
                )
                for i in range(2)
            ]
            outs.append(jnp.where(half, both[0], both[1]))
        return jnp.concatenate(outs, axis=0)[:live_rows]

    wait(recv_sem.at[G_VEC], vg.at[pl.ds(0, ng - 1)])
    row_vectors = jnp.dot(
        row_sel, vg[...].reshape(slab_rows, TILE), preferred_element_type=jnp.float32
    )
    locals_[4].wait()
    cprod[y, 0:live_rows, :] = apply(row_vectors, 0)
    mine = cprod.at[y, pl.ds(0, live_rows)]
    send_all(Y_PROD, y_peer, ny, lambda p: mine, mine)

    wait(recv_sem.at[Y_VEC], yrecv.at[pl.ds(0, ny - 1)])
    col_vectors = yrecv[0].astype(jnp.float32)
    for p in range(1, ny):
        col_vectors = col_vectors + yrecv[p].astype(jnp.float32)
    rprod[g, 0:live_rows, :] = apply(col_vectors, 1)
    mine_r = rprod.at[g, pl.ds(0, live_rows)]
    send_all(G_PROD, g_peer, ng, lambda p: mine_r, mine_r)

    col_place = col_sel.T[: nz * ROWS].astype(jnp.bfloat16)
    wait(recv_sem.at[G_CODE], rcode.at[pl.ds(0, ng - 1)])
    row_place = jnp.concatenate(
        [
            onehot(widen(lambda s, p=p: rcode[p, s : s + 1, :]), g * (nh * ROWS))
            for p in range(ng)
        ],
        axis=0,
    ).T[: nh * ROWS].astype(jnp.bfloat16)

    wait(recv_sem.at[Y_PROD], cprod.at[pl.ds(0, ny - 1), pl.ds(0, live_rows)])
    sums = place(col_place, cprod[...].reshape(ny * SLOT_ROWS, TILE))
    zsend[...] = sums.reshape(nz, ROWS, TILE)
    send_all(Z_PROD, z_peer, nz, lambda p: zsend.at[p], zrecv.at[z])
    zrecv[z] = zsend[z]

    wait(recv_sem.at[G_PROD], rprod.at[pl.ds(0, ng - 1), pl.ds(0, live_rows)])
    sums = place(row_place, rprod[...].reshape(ng * SLOT_ROWS, TILE))
    hsend[...] = sums.reshape(nh, ROWS, TILE)
    send(H_PROD, hsend.at[h_other], hrecv, h_id)
    total = hsend[h]

    wait(recv_sem.at[H_PROD], hrecv)
    total = total + hrecv[...]
    wait(recv_sem.at[Z_PROD], zrecv.at[pl.ds(0, nz - 1)])
    for p in range(nz):
        total = total + zrecv[p]
    for j in range(VB):
        out_ref[j] = total[NVEC * j : NVEC * (j + 1), :]

    wait(send_sem.at[H_VEC], hsend_like(vh))
    wait(send_sem.at[G_CODE], rcode.at[pl.ds(0, ng - 1)])
    wait(send_sem.at[Y_CODE], ccode.at[pl.ds(0, ny - 1)])
    wait(send_sem.at[Z_VEC], vz.at[pl.ds(0, nz - 1)])
    wait(send_sem.at[G_VEC], vg.at[pl.ds(0, ng - 1)])
    wait(send_sem.at[Y_VEC], ysend.at[pl.ds(0, ny - 1)])
    wait(send_sem.at[Y_PROD], cprod.at[pl.ds(0, ny - 1), pl.ds(0, live_rows)])
    wait(send_sem.at[G_PROD], rprod.at[pl.ds(0, ng - 1), pl.ds(0, live_rows)])
    wait(send_sem.at[Z_PROD], zsend.at[pl.ds(0, nz - 1)])
    wait(send_sem.at[H_PROD], hrecv)


def hsend_like(ref):
    return ref.at[0]


def on_device(sizes, vectors, tiles, tile_rows, tile_cols, tile_counts):
    ny, nz, nx, nh, nc = sizes
    ng = nx * nc
    slots = tiles.shape[2]
    bf16, f32, i32 = jnp.bfloat16, jnp.float32, jnp.int32
    vmem, smem = pltpu.VMEM, pltpu.SMEM
    return pl.pallas_call(
        functools.partial(kernel, sizes),
        out_shape=jax.ShapeDtypeStruct(vectors.shape, f32),
        in_specs=[pl.BlockSpec(memory_space=pltpu.HBM)] * 5,
        out_specs=pl.BlockSpec(memory_space=pltpu.VMEM),
        scratch_shapes=[
            vmem(vectors.shape, bf16),
            vmem(tiles.shape[2:], bf16),
            smem(tile_rows.shape, i32),
            smem(tile_cols.shape, i32),
            smem(tile_counts.shape, i32),
            vmem((nz, ROWS, TILE), bf16),
            vmem((nh, ROWS, TILE), bf16),
            vmem((ng, nh * ROWS, TILE), bf16),
            vmem((ny, PAD, LANES), i32),
            vmem((ng, PAD, LANES), i32),
            vmem((ny, SLOT_ROWS, TILE), bf16),
            vmem((ny, SLOT_ROWS, TILE), bf16),
            vmem((ny, SLOT_ROWS, TILE), f32),
            vmem((ng, SLOT_ROWS, TILE), f32),
            vmem((nz, ROWS, TILE), f32),
            vmem((nz, ROWS, TILE), f32),
            vmem((nh, ROWS, TILE), f32),
            vmem((ROWS, TILE), f32),
            pltpu.SemaphoreType.DMA((5,)),
            pltpu.SemaphoreType.DMA((10,)),
            pltpu.SemaphoreType.DMA((10,)),
        ],
        compiler_params=pltpu.CompilerParams(
            collective_id=0, has_side_effects=True, vmem_limit_bytes=60 * 2**20
        ),
        cost_estimate=pl.CostEstimate(
            flops=2**24, bytes_accessed=2**20, transcendentals=0
        ),
    )(vectors, tiles, tile_rows, tile_cols, tile_counts)


def build(mesh, nz, nh, nc):
    ny, nx = mesh.shape["row"] // nz, mesh.shape["col"] // (nh * nc)
    placed = (
        P(("row", "col"), None, None),
        P("row", "col", None, None, None),
        P("row", "col", None),
        P("row", "col", None),
        P("row", "col"),
    )
    return jax.shard_map(
        functools.partial(on_device, (ny, nz, nx, nh, nc)),
        mesh=mesh,
        in_specs=placed,
        out_specs=P(("row", "col"), None, None),
        check_vma=False,
    )


def solution(mesh):
    return build(mesh, 8, 2, 2)
```

time: 1420 us -> 54.9 us (0.04)
  the two profiles are of different devices: /device:TPU:2 before, /device:TPU:128 now
where the time goes in v1:
time: 54.9 us; the launch traced here: 54.6 us
  Pallas kernels  52.6 us (96%)
  local copies, waits for them, and re-layouts  1.32 us (2%)
  between operations  0.66 us (1%)
    pallas_call x1, Pallas kernels, on_device(): pl.pallas_call(functools.partial(kernel, sizes), out_shape=jax.ShapeDtype...  52.6 us
    unnamed x1, local copies, waits for them, and re-layouts  1.32 us

profile of v1, /device:TPU:128, one launch (start us, length us, event | category | flops | bytes accessed | tf_op | source)
XLA Modules:
  0.0 54.6 jit_solution(3770876120759319002)
XLA Ops:
  0.7 52.6 %shard_map.55 = f32[4,4,256]{2,1,0:T(4,128)} custom-call(bf16[4,4,256]{2,1,0:T(4,128)(2,1)} %vec_hbm.1, bf16[1,1,6,256,256]{4,3,2,1,0:T(8,128)(2,1)} %tiles_hbm.1, s32[1,1,6]{2,1,0:T(1,128)} %rows_hbm.1, s32[1,1,6]{2,1,0:T(1,128)} %cols_hbm.1, s32[1,1]{1,0:T(1,128)S(6)} %copy.7.counts_hbm), custom_call_target="tpu_custom_call" | custom-call | flops 16777216 | bytes 1048576 | tf_op jit(solution)/shard_map/pallas_call | solution.py:272
  53.3 1.3 %copy.8 = f32[4,4,256]{2,1,0:T(4,128)} copy(f32[4,4,256]{2,1,0:T(4,128)} %shard_map.55) | data formatting | bytes 32768

commit v2 on v1

v2 whole, which is shorter than its diff:
```python
import functools

import jax
import jax.numpy as jnp
from jax import lax
from jax.experimental import pallas as pl
from jax.experimental.pallas import tpu as pltpu
from jax.sharding import PartitionSpec as P

MESH = pl.DeviceIdType.MESH
NVEC = 4
TILE = 256
VB = 4
ROWS = VB * NVEC
PAD = 8
SLOT_ROWS = PAD * NVEC
LANES = 128
NONE = -(2**20)

H_VEC, X_CODE, Y_CODE, Z_VEC, X_VEC, Y_VEC, Y_PROD, X_PROD, Z_PROD, H_PROD = range(10)


def widen(row_of):
    sub = lax.broadcasted_iota(jnp.int32, (8, LANES), 0)
    pieces = []
    for k in range(PAD // 2):
        low = jnp.broadcast_to(row_of(2 * k), (8, LANES))
        high = jnp.broadcast_to(row_of(2 * k + 1), (8, LANES))
        pieces.append(jnp.where(sub < 4, low, high) + (sub & 3))
    return jnp.concatenate(pieces, axis=0)


def onehot(codes, base):
    lane = lax.broadcasted_iota(jnp.int32, codes.shape, 1)
    return jnp.where(codes == lane + base, 1.0, 0.0).astype(jnp.float32)


def place(matrix, products):
    high = products.astype(jnp.bfloat16)
    low = (products - high.astype(jnp.float32)).astype(jnp.bfloat16)
    return jnp.dot(matrix, high, preferred_element_type=jnp.float32) + jnp.dot(
        matrix, low, preferred_element_type=jnp.float32
    )


def kernel(
    sizes,
    vec_hbm, tiles_hbm, rows_hbm, cols_hbm, counts_hbm,
    out_ref,
    vin, tiles, rows_s, cols_s, counts_s,
    vz, vw, vx, ccode, rcode, ysend, yrecv, cprod, rprod, zsend, zrecv, wsend, wrecv, col_place,
    local_sem, send_sem, recv_sem,
):
    ny, nz, nx, nh, nc = sizes
    nw = nh * nc
    slots = tiles.shape[0]
    live_rows = slots * NVEC
    row, col = lax.axis_index("row"), lax.axis_index("col")
    y, z = row // nz, row % nz
    x, w = col // nw, col % nw
    h = w // nc

    def at(y_, z_, x_, w_):
        return (y_ * nz + z_, x_ * nw + w_)

    def peers(me, n, place_of):
        out = []
        for k in sorted(range(1, n), key=lambda k: -min(k, n - k)):
            p = lax.rem(me + k, n)
            out.append((p, place_of(p)))
        return out

    y_peers = peers(y, ny, lambda p: at(p, z, x, w))
    z_peers = peers(z, nz, lambda p: at(y, p, x, w))
    x_peers = peers(x, nx, lambda p: at(y, z, p, w))
    w_peers = peers(w, nw, lambda p: at(y, z, x, p))

    locals_ = [
        pltpu.make_async_copy(src, dst, local_sem.at[i])
        for i, (src, dst) in enumerate(
            (
                (vec_hbm, vin),
                (rows_hbm, rows_s),
                (cols_hbm, cols_s),
                (counts_hbm, counts_s),
                (tiles_hbm.at[0, 0], tiles),
            )
        )
    ]
    locals_[0].start()
    barrier = pltpu.get_barrier_semaphore()
    everyone = [device_id for _, device_id in w_peers + z_peers + y_peers + x_peers]
    for device_id in everyone:
        pl.semaphore_signal(barrier, inc=1, device_id=device_id, device_id_type=MESH)
    for copy in locals_[1:]:
        copy.start()

    def send(which, src, dst, device_id):
        pltpu.make_async_remote_copy(
            src_ref=src,
            dst_ref=dst,
            send_sem=send_sem.at[which],
            recv_sem=recv_sem.at[which],
            device_id=device_id,
            device_id_type=MESH,
        ).start()

    def wait(sem, ref):
        pltpu.make_async_copy(ref, ref, sem).wait()

    def send_all(which, peers_, src_of, dst):
        for p, device_id in peers_:
            send(which, src_of(p), dst, device_id)

    tail = SLOT_ROWS - live_rows
    if tail:
        cprod[:, live_rows:, :] = jnp.zeros((ny, tail, TILE), jnp.float32)
        rprod[:, live_rows:, :] = jnp.zeros((nx, tail, TILE), jnp.float32)

    locals_[0].wait()
    own = jnp.concatenate([vin[j].astype(jnp.float32) for j in range(VB)], axis=0)
    own = own.astype(jnp.bfloat16)
    vz[z] = own
    vw[w] = own
    for i in (1, 2, 3):
        locals_[i].wait()
    live = counts_s[0, 0]
    sub = lax.broadcasted_iota(jnp.int32, (PAD, LANES), 0)
    col_codes = jnp.full((PAD, LANES), NONE, jnp.int32)
    row_codes = col_codes
    for s in range(slots):
        q = cols_s[0, 0, s] * NVEC
        p = rows_s[0, 0, s] * NVEC
        col_codes = jnp.where(sub == s, jnp.where(s < live, q, NONE), col_codes)
        row_codes = jnp.where(sub == s, jnp.where(s < live, p, NONE), row_codes)
    ccode[y] = col_codes
    rcode[x] = row_codes

    own_row_codes = widen(lambda s: row_codes[s : s + 1, :])
    slab_rows = nx * nw * ROWS
    pieces = [
        onehot(own_row_codes, b)[:, : min(LANES, slab_rows - b)]
        for b in range(0, slab_rows, LANES)
    ]
    row_sel = jnp.concatenate(pieces, axis=1).astype(jnp.bfloat16)
    half = lax.broadcasted_iota(jnp.int32, (8, TILE), 0) < 4

    def apply(vectors, contract):
        outs = []
        for k in range((slots + 1) // 2):
            pair = vectors[8 * k : 8 * k + 8].astype(jnp.bfloat16)
            both = [
                lax.dot_general(
                    pair,
                    tiles[min(2 * k + i, slots - 1)],
                    (((1,), (contract,)), ((), ())),
                    preferred_element_type=jnp.float32,
                )
                for i in range(2)
            ]
            outs.append(jnp.where(half, both[0], both[1]))
        return jnp.concatenate(outs, axis=0)[:live_rows]

    pl.semaphore_wait(barrier, len(everyone))

    send_all(H_VEC, w_peers, lambda p: vw.at[w], vw.at[w])
    send_all(Z_VEC, z_peers, lambda p: vz.at[z], vz.at[z])
    send_all(Y_CODE, y_peers, lambda p: ccode.at[y], ccode.at[y])
    send_all(X_CODE, x_peers, lambda p: rcode.at[x], rcode.at[x])

    def slab_vectors():
        wait(recv_sem.at[H_VEC], vw.at[pl.ds(0, nw - 1)])
        vx[x] = vw[...].reshape(nw * ROWS, TILE)
        send_all(X_VEC, x_peers, lambda p: vx.at[x], vx.at[x])

    def column_products():
        wait(recv_sem.at[X_VEC], vx.at[pl.ds(0, nx - 1)])
        row_vectors = jnp.dot(
            row_sel, vx[...].reshape(slab_rows, TILE), preferred_element_type=jnp.float32
        )
        cprod[y, 0:live_rows, :] = apply(row_vectors, 0)
        mine = cprod.at[y, pl.ds(0, live_rows)]
        send_all(Y_PROD, y_peers, lambda p: mine, mine)

    def column_sums():
        wait(recv_sem.at[Y_PROD], cprod.at[pl.ds(0, ny - 1), pl.ds(0, live_rows)])
        sums = place(col_place[...], cprod[...].reshape(ny * SLOT_ROWS, TILE))
        zsend[...] = sums.reshape(nz, ROWS, TILE)
        send_all(Z_PROD, z_peers, lambda p: zsend.at[p], zrecv.at[z])
        zrecv[z] = zsend[z]

    columns_first = h == 0

    pl.when(columns_first)(slab_vectors)

    wait(recv_sem.at[Y_CODE], ccode.at[pl.ds(0, ny - 1)])
    col_sel = jnp.concatenate(
        [
            onehot(widen(lambda s, p=p: ccode[p, s : s + 1, :]), y * (nz * ROWS))
            for p in range(ny)
        ],
        axis=0,
    )
    wait(recv_sem.at[Z_VEC], vz.at[pl.ds(0, nz - 1)])
    plane = vz[...].reshape(nz * ROWS, TILE)
    picked = jnp.dot(
        col_sel[:, : nz * ROWS].astype(jnp.bfloat16), plane, preferred_element_type=jnp.float32
    )
    ysend[...] = picked.astype(jnp.bfloat16).reshape(ny, SLOT_ROWS, TILE)
    send_all(Y_VEC, y_peers, lambda p: ysend.at[p], yrecv.at[y])
    yrecv[y] = ysend[y]

    pl.when(jnp.logical_not(columns_first))(slab_vectors)

    wait(recv_sem.at[X_CODE], rcode.at[pl.ds(0, nx - 1)])
    row_place = jnp.concatenate(
        [
            onehot(widen(lambda s, p=p: rcode[p, s : s + 1, :]), x * (nw * ROWS))
            for p in range(nx)
        ],
        axis=0,
    ).T[: nw * ROWS].astype(jnp.bfloat16)
    col_place[...] = col_sel.T[: nz * ROWS].astype(jnp.bfloat16)
    locals_[4].wait()

    pl.when(columns_first)(column_products)

    wait(recv_sem.at[Y_VEC], yrecv.at[pl.ds(0, ny - 1)])
    col_vectors = yrecv[0].astype(jnp.float32)
    for p in range(1, ny):
        col_vectors = col_vectors + yrecv[p].astype(jnp.float32)
    rprod[x, 0:live_rows, :] = apply(col_vectors, 1)
    mine_r = rprod.at[x, pl.ds(0, live_rows)]
    send_all(X_PROD, x_peers, lambda p: mine_r, mine_r)

    pl.when(jnp.logical_not(columns_first))(column_products)

    pl.when(columns_first)(column_sums)

    wait(recv_sem.at[X_PROD], rprod.at[pl.ds(0, nx - 1), pl.ds(0, live_rows)])
    sums = place(row_place, rprod[...].reshape(nx * SLOT_ROWS, TILE))
    wsend[...] = sums.reshape(nw, ROWS, TILE)
    send_all(H_PROD, w_peers, lambda p: wsend.at[p], wrecv.at[w])
    wrecv[w] = wsend[w]

    pl.when(jnp.logical_not(columns_first))(column_sums)

    wait(recv_sem.at[H_PROD], wrecv.at[pl.ds(0, nw - 1)])
    total = wrecv[0]
    for p in range(1, nw):
        total = total + wrecv[p]
    wait(recv_sem.at[Z_PROD], zrecv.at[pl.ds(0, nz - 1)])
    for p in range(nz):
        total = total + zrecv[p]
    for j in range(VB):
        out_ref[j] = total[NVEC * j : NVEC * (j + 1), :]

    wait(send_sem.at[H_VEC], vw.at[pl.ds(0, nw - 1)])
    wait(send_sem.at[X_CODE], rcode.at[pl.ds(0, nx - 1)])
    wait(send_sem.at[Y_CODE], ccode.at[pl.ds(0, ny - 1)])
    wait(send_sem.at[Z_VEC], vz.at[pl.ds(0, nz - 1)])
    wait(send_sem.at[X_VEC], vx.at[pl.ds(0, nx - 1)])
    wait(send_sem.at[Y_VEC], ysend.at[pl.ds(0, ny - 1)])
    wait(send_sem.at[Y_PROD], cprod.at[pl.ds(0, ny - 1), pl.ds(0, live_rows)])
    wait(send_sem.at[X_PROD], rprod.at[pl.ds(0, nx - 1), pl.ds(0, live_rows)])
    wait(send_sem.at[Z_PROD], zsend.at[pl.ds(0, nz - 1)])
    wait(send_sem.at[H_PROD], wsend.at[pl.ds(0, nw - 1)])


def on_device(sizes, vectors, tiles, tile_rows, tile_cols, tile_counts):
    ny, nz, nx, nh, nc = sizes
    nw = nh * nc
    bf16, f32, i32 = jnp.bfloat16, jnp.float32, jnp.int32
    vmem, smem = pltpu.VMEM, pltpu.SMEM
    return pl.pallas_call(
        functools.partial(kernel, sizes),
        out_shape=jax.ShapeDtypeStruct(vectors.shape, f32),
        in_specs=[pl.BlockSpec(memory_space=pltpu.HBM)] * 5,
        out_specs=pl.BlockSpec(memory_space=pltpu.VMEM),
        scratch_shapes=[
            vmem(vectors.shape, bf16),
            vmem(tiles.shape[2:], bf16),
            smem(tile_rows.shape, i32),
            smem(tile_cols.shape, i32),
            smem(tile_counts.shape, i32),
            vmem((nz, ROWS, TILE), bf16),
            vmem((nw, ROWS, TILE), bf16),
            vmem((nx, nw * ROWS, TILE), bf16),
            vmem((ny, PAD, LANES), i32),
            vmem((nx, PAD, LANES), i32),
            vmem((ny, SLOT_ROWS, TILE), bf16),
            vmem((ny, SLOT_ROWS, TILE), bf16),
            vmem((ny, SLOT_ROWS, TILE), f32),
            vmem((nx, SLOT_ROWS, TILE), f32),
            vmem((nz, ROWS, TILE), f32),
            vmem((nz, ROWS, TILE), f32),
            vmem((nw, ROWS, TILE), f32),
            vmem((nw, ROWS, TILE), f32),
            vmem((nz * ROWS, ny * SLOT_ROWS), bf16),
            pltpu.SemaphoreType.DMA((5,)),
            pltpu.SemaphoreType.DMA((10,)),
            pltpu.SemaphoreType.DMA((10,)),
        ],
        compiler_params=pltpu.CompilerParams(
            collective_id=0, has_side_effects=True, vmem_limit_bytes=55000 * 2**10
        ),
        cost_estimate=pl.CostEstimate(
            flops=2**24, bytes_accessed=2**20, transcendentals=0
        ),
    )(vectors, tiles, tile_rows, tile_cols, tile_counts)


def build(mesh, nz, nh, nc):
    ny, nx = mesh.shape["row"] // nz, mesh.shape["col"] // (nh * nc)
    placed = (
        P(("row", "col"), None, None),
        P("row", "col", None, None, None),
        P("row", "col", None),
        P("row", "col", None),
        P("row", "col"),
    )
    return jax.shard_map(
        functools.partial(on_device, (ny, nz, nx, nh, nc)),
        mesh=mesh,
        in_specs=placed,
        out_specs=P(("row", "col"), None, None),
        check_vma=False,
    )


def solution(mesh):
    return build(mesh, 8, 2, 2)
```

time: 54.9 us -> 51.1 us (0.931)
  the two profiles are of different devices: /device:TPU:128 before, /device:TPU:2 now
where the time goes in v2:
time: 51.1 us; the launch traced here: 50.9 us
  Pallas kernels  48.9 us (96%)
  local copies, waits for them, and re-layouts  1.31 us (3%)
  between operations  0.71 us (1%)
    pallas_call x1, Pallas kernels, on_device(): pl.pallas_call(functools.partial(kernel, sizes), out_shape=jax.ShapeDtype...  48.9 us
    unnamed x7, local copies, waits for them, and re-layouts  1.31 us

profile of v2, /device:TPU:2, one launch (start us, length us, event | category | flops | bytes accessed | tf_op | source)
XLA Modules:
  0.0 50.9 jit_solution(8565554641368248826)
XLA Ops:
  0.0 0.0 copy-start.2
  0.0 0.0 copy-start.1
  0.7 0.0 copy-done.2
  0.7 0.0 copy-done.1
  0.7 0.0 copy-start
  0.7 0.7 %copy-done = bf16[4,4,256]{2,1,0:T(4,128)(2,1)S(1)} copy-done((bf16[4,4,256]{2,1,0:T(4,128)(2,1)S(1)}, bf16[4,4,256]{2,1,0:T(4,128)(2,1)}, u32[]{:S(2)}) %copy-start) | copy-done | bytes 8216
  1.4 48.9 %shard_map.55 = f32[4,4,256]{2,1,0:T(4,128)S(1)} custom-call(bf16[4,4,256]{2,1,0:T(4,128)(2,1)S(1)} %copy-done, bf16[1,1,6,256,256]{4,3,2,1,0:T(8,128)(2,1)} %tiles_hbm.1, s32[1,1,6]{2,1,0:T(1,128)S(1)} %copy-done.1, s32[1,1,6]{2,1,0:T(1,128)S(1)} %copy-done.2, s32[1,1]{1,0:T(1,128)S(6)} %copy.7.counts_hbm), custom_call_target="tpu_custom_call" | custom-call | flops 16777216 | bytes 1048576 | tf_op jit(solution)/shard_map/pallas_call | solution.py:275
  50.3 0.6 %copy.8 = f32[4,4,256]{2,1,0:T(4,128)} copy(f32[4,4,256]{2,1,0:T(4,128)S(1)} %shard_map.55) | data formatting | bytes 32768
Async XLA Ops:
  0.0 0.7 %copy-start.2 = (s32[1,1,6]{2,1,0:T(1,128)S(1)}, s32[1,1,6]{2,1,0:T(1,128)}, u32[]{:S(2)}) copy-start(s32[1,1,6]{2,1,0:T(1,128)} %cols_hbm.1) | copy-start | bytes 76
  0.0 0.7 %copy-start.1 = (s32[1,1,6]{2,1,0:T(1,128)S(1)}, s32[1,1,6]{2,1,0:T(1,128)}, u32[]{:S(2)}) copy-start(s32[1,1,6]{2,1,0:T(1,128)} %rows_hbm.1) | copy-start | bytes 76
  0.7 0.7 %copy-start = (bf16[4,4,256]{2,1,0:T(4,128)(2,1)S(1)}, bf16[4,4,256]{2,1,0:T(4,128)(2,1)}, u32[]{:S(2)}) copy-start(bf16[4,4,256]{2,1,0:T(4,128)(2,1)} %vec_hbm.1) | copy-start | bytes 24580

commit v3 on v2

--- a/solution.py
+++ b/solution.py
@@ -17,7 +17,9 @@
 LANES = 128
 NONE = -(2**20)
 
-H_VEC, X_CODE, Y_CODE, Z_VEC, X_VEC, Y_VEC, Y_PROD, X_PROD, Z_PROD, H_PROD = range(10)
+GROUPS = 13
+H_VEC, X_CODE, Y_CODE, Z_CODE, Z_VEC, X_VEC, Y_VEC = range(7)
+Y_PROD, Z_SUM, Z_PROD, Y_SUM, X_PROD, H_PROD = range(7, GROUPS)
 
 
 def widen(row_of):
@@ -30,9 +32,10 @@
     return jnp.concatenate(pieces, axis=0)
 
 
-def onehot(codes, base):
+def onehot(codes, base, gap=0):
     lane = lax.broadcasted_iota(jnp.int32, codes.shape, 1)
-    return jnp.where(codes == lane + base, 1.0, 0.0).astype(jnp.float32)
+    target = lane + base + (lane // ROWS) * gap
+    return jnp.where(codes == target, 1.0, 0.0).astype(jnp.float32)
 
 
 def place(matrix, products):
@@ -48,7 +51,8 @@
     vec_hbm, tiles_hbm, rows_hbm, cols_hbm, counts_hbm,
     out_ref,
     vin, tiles, rows_s, cols_s, counts_s,
-    vz, vw, vx, ccode, rcode, ysend, yrecv, cprod, rprod, zsend, zrecv, wsend, wrecv, col_place,
+    vz, vw, vx, ccode, zcode, rcode, ysend, yrecv, yprod, zprod, rprod,
+    zsend, zrecv, ssend, srecv, wsend, wrecv, y_place, z_place,
     local_sem, send_sem, recv_sem,
 ):
     ny, nz, nx, nh, nc = sizes
@@ -114,7 +118,8 @@
 
     tail = SLOT_ROWS - live_rows
     if tail:
-        cprod[:, live_rows:, :] = jnp.zeros((ny, tail, TILE), jnp.float32)
+        yprod[:, live_rows:, :] = jnp.zeros((ny, tail, LANES), jnp.float32)
+        zprod[:, live_rows:, :] = jnp.zeros((nz, tail, LANES), jnp.float32)
         rprod[:, live_rows:, :] = jnp.zeros((nx, tail, TILE), jnp.float32)
 
     locals_[0].wait()
@@ -134,6 +139,7 @@
         col_codes = jnp.where(sub == s, jnp.where(s < live, q, NONE), col_codes)
         row_codes = jnp.where(sub == s, jnp.where(s < live, p, NONE), row_codes)
     ccode[y] = col_codes
+    zcode[z] = col_codes
     rcode[x] = row_codes
 
     own_row_codes = widen(lambda s: row_codes[s : s + 1, :])
@@ -178,16 +184,25 @@
         row_vectors = jnp.dot(
             row_sel, vx[...].reshape(slab_rows, TILE), preferred_element_type=jnp.float32
         )
-        cprod[y, 0:live_rows, :] = apply(row_vectors, 0)
-        mine = cprod.at[y, pl.ds(0, live_rows)]
-        send_all(Y_PROD, y_peers, lambda p: mine, mine)
+        products = apply(row_vectors, 0)
+        zprod[z, 0:live_rows, :] = products[:, LANES:]
+        mine_z = zprod.at[z, pl.ds(0, live_rows)]
+        send_all(Z_PROD, z_peers, lambda p: mine_z, mine_z)
+        yprod[y, 0:live_rows, :] = products[:, :LANES]
+        mine_y = yprod.at[y, pl.ds(0, live_rows)]
+        send_all(Y_PROD, y_peers, lambda p: mine_y, mine_y)
 
     def column_sums():
-        wait(recv_sem.at[Y_PROD], cprod.at[pl.ds(0, ny - 1), pl.ds(0, live_rows)])
-        sums = place(col_place[...], cprod[...].reshape(ny * SLOT_ROWS, TILE))
-        zsend[...] = sums.reshape(nz, ROWS, TILE)
-        send_all(Z_PROD, z_peers, lambda p: zsend.at[p], zrecv.at[z])
+        wait(recv_sem.at[Y_PROD], yprod.at[pl.ds(0, ny - 1), pl.ds(0, live_rows)])
+        sums = place(y_place[...], yprod[...].reshape(ny * SLOT_ROWS, LANES))
+        zsend[...] = sums.reshape(nz, ROWS, LANES)
+        send_all(Z_SUM, z_peers, lambda p: zsend.at[p], zrecv.at[z])
         zrecv[z] = zsend[z]
+        wait(recv_sem.at[Z_PROD], zprod.at[pl.ds(0, nz - 1), pl.ds(0, live_rows)])
+        sums = place(z_place[...], zprod[...].reshape(nz * SLOT_ROWS, LANES))
+        ssend[...] = sums.reshape(ny, ROWS, LANES)
+        send_all(Y_SUM, y_peers, lambda p: ssend.at[p], srecv.at[y])
+        srecv[y] = ssend[y]
 
     columns_first = h == 0
 
@@ -206,9 +221,13 @@
     picked = jnp.dot(
         col_sel[:, : nz * ROWS].astype(jnp.bfloat16), plane, preferred_element_type=jnp.float32
     )
-    ysend[...] = picked.astype(jnp.bfloat16).reshape(ny, SLOT_ROWS, TILE)
+    for p in range(ny):
+        some = picked[SLOT_ROWS * p : SLOT_ROWS * p + live_rows]
+        both = jnp.concatenate([some[:, :LANES], some[:, LANES:]], axis=0)
+        ysend[p] = both.astype(jnp.bfloat16)
     send_all(Y_VEC, y_peers, lambda p: ysend.at[p], yrecv.at[y])
     yrecv[y] = ysend[y]
+    send_all(Z_CODE, z_peers, lambda p: zcode.at[z], zcode.at[z])
 
     pl.when(jnp.logical_not(columns_first))(slab_vectors)
 
@@ -220,7 +239,7 @@
         ],
         axis=0,
     ).T[: nw * ROWS].astype(jnp.bfloat16)
-    col_place[...] = col_sel.T[: nz * ROWS].astype(jnp.bfloat16)
+    y_place[...] = col_sel.T[: nz * ROWS].astype(jnp.bfloat16)
     locals_[4].wait()
 
     pl.when(columns_first)(column_products)
@@ -229,11 +248,21 @@
     col_vectors = yrecv[0].astype(jnp.float32)
     for p in range(1, ny):
         col_vectors = col_vectors + yrecv[p].astype(jnp.float32)
+    col_vectors = jnp.concatenate([col_vectors[:live_rows], col_vectors[live_rows:]], axis=1)
     rprod[x, 0:live_rows, :] = apply(col_vectors, 1)
     mine_r = rprod.at[x, pl.ds(0, live_rows)]
     send_all(X_PROD, x_peers, lambda p: mine_r, mine_r)
 
     pl.when(jnp.logical_not(columns_first))(column_products)
+
+    wait(recv_sem.at[Z_CODE], zcode.at[pl.ds(0, nz - 1)])
+    z_place[...] = jnp.concatenate(
+        [
+            onehot(widen(lambda s, p=p: zcode[p, s : s + 1, :]), z * ROWS, (nz - 1) * ROWS)
+            for p in range(nz)
+        ],
+        axis=0,
+    ).T[: ny * ROWS].astype(jnp.bfloat16)
 
     pl.when(columns_first)(column_sums)
 
@@ -249,9 +278,15 @@
     total = wrecv[0]
     for p in range(1, nw):
         total = total + wrecv[p]
-    wait(recv_sem.at[Z_PROD], zrecv.at[pl.ds(0, nz - 1)])
-    for p in range(nz):
-        total = total + zrecv[p]
+    wait(recv_sem.at[Y_SUM], srecv.at[pl.ds(0, ny - 1)])
+    right = srecv[0]
+    for p in range(1, ny):
+        right = right + srecv[p]
+    wait(recv_sem.at[Z_SUM], zrecv.at[pl.ds(0, nz - 1)])
+    left = zrecv[0]
+    for p in range(1, nz):
+        left = left + zrecv[p]
+    total = total + jnp.concatenate([left, right], axis=1)
     for j in range(VB):
         out_ref[j] = total[NVEC * j : NVEC * (j + 1), :]
 
@@ -261,15 +296,19 @@
     wait(send_sem.at[Z_VEC], vz.at[pl.ds(0, nz - 1)])
     wait(send_sem.at[X_VEC], vx.at[pl.ds(0, nx - 1)])
     wait(send_sem.at[Y_VEC], ysend.at[pl.ds(0, ny - 1)])
-    wait(send_sem.at[Y_PROD], cprod.at[pl.ds(0, ny - 1), pl.ds(0, live_rows)])
+    wait(send_sem.at[Z_CODE], zcode.at[pl.ds(0, nz - 1)])
+    wait(send_sem.at[Y_PROD], yprod.at[pl.ds(0, ny - 1), pl.ds(0, live_rows)])
+    wait(send_sem.at[Z_PROD], zprod.at[pl.ds(0, nz - 1), pl.ds(0, live_rows)])
     wait(send_sem.at[X_PROD], rprod.at[pl.ds(0, nx - 1), pl.ds(0, live_rows)])
-    wait(send_sem.at[Z_PROD], zsend.at[pl.ds(0, nz - 1)])
+    wait(send_sem.at[Z_SUM], zsend.at[pl.ds(0, nz - 1)])
+    wait(send_sem.at[Y_SUM], ssend.at[pl.ds(0, ny - 1)])
     wait(send_sem.at[H_PROD], wsend.at[pl.ds(0, nw - 1)])
 
 
 def on_device(sizes, vectors, tiles, tile_rows, tile_cols, tile_counts):
     ny, nz, nx, nh, nc = sizes
     nw = nh * nc
+    live_rows = tiles.shape[2] * NVEC
     bf16, f32, i32 = jnp.bfloat16, jnp.float32, jnp.int32
     vmem, smem = pltpu.VMEM, pltpu.SMEM
     return pl.pallas_call(
@@ -287,19 +326,24 @@
             vmem((nw, ROWS, TILE), bf16),
             vmem((nx, nw * ROWS, TILE), bf16),
             vmem((ny, PAD, LANES), i32),
+            vmem((nz, PAD, LANES), i32),
             vmem((nx, PAD, LANES), i32),
-            vmem((ny, SLOT_ROWS, TILE), bf16),
-            vmem((ny, SLOT_ROWS, TILE), bf16),
-            vmem((ny, SLOT_ROWS, TILE), f32),
+            vmem((ny, 2 * live_rows, LANES), bf16),
+            vmem((ny, 2 * live_rows, LANES), bf16),
+            vmem((ny, SLOT_ROWS, LANES), f32),
+            vmem((nz, SLOT_ROWS, LANES), f32),
             vmem((nx, SLOT_ROWS, TILE), f32),
-            vmem((nz, ROWS, TILE), f32),
-            vmem((nz, ROWS, TILE), f32),
+            vmem((nz, ROWS, LANES), f32),
+            vmem((nz, ROWS, LANES), f32),
+            vmem((ny, ROWS, LANES), f32),
+            vmem((ny, ROWS, LANES), f32),
             vmem((nw, ROWS, TILE), f32),
             vmem((nw, ROWS, TILE), f32),
             vmem((nz * ROWS, ny * SLOT_ROWS), bf16),
+            vmem((ny * ROWS, nz * SLOT_ROWS), bf16),
             pltpu.SemaphoreType.DMA((5,)),
-            pltpu.SemaphoreType.DMA((10,)),
-            pltpu.SemaphoreType.DMA((10,)),
+            pltpu.SemaphoreType.DMA((GROUPS,)),
+            pltpu.SemaphoreType.DMA((GROUPS,)),
         ],
         compiler_params=pltpu.CompilerParams(
             collective_id=0, has_side_effects=True, vmem_limit_bytes=55000 * 2**10

time: 51.1 us -> 48.2 us (0.943)
  the two profiles are of different devices: /device:TPU:2 before, /device:TPU:1 now
where the time goes in v3:
time: 48.2 us; the launch traced here: 48 us
  Pallas kernels  46 us (95%)
  local copies, waits for them, and re-layouts  1.31 us (3%)
  between operations  0.71 us (1%)
    pallas_call x1, Pallas kernels, on_device(): pl.pallas_call(functools.partial(kernel, sizes), out_shape=jax.ShapeDtype...  46 us
    unnamed x7, local copies, waits for them, and re-layouts  1.31 us

profile of v3, /device:TPU:1, one launch (start us, length us, event | category | flops | bytes accessed | tf_op | source)
XLA Modules:
  0.0 48.0 jit_solution(5856730153704388653)
XLA Ops:
  0.0 0.0 copy-start.2
  0.0 0.0 copy-start.1
  0.7 0.0 copy-done.2
  0.7 0.0 copy-done.1
  0.7 0.0 copy-start
  0.7 0.7 %copy-done = bf16[4,4,256]{2,1,0:T(4,128)(2,1)S(1)} copy-done((bf16[4,4,256]{2,1,0:T(4,128)(2,1)S(1)}, bf16[4,4,256]{2,1,0:T(4,128)(2,1)}, u32[]{:S(2)}) %copy-start) | copy-done | bytes 8216
  1.4 46.0 %shard_map.55 = f32[4,4,256]{2,1,0:T(4,128)S(1)} custom-call(bf16[4,4,256]{2,1,0:T(4,128)(2,1)S(1)} %copy-done, bf16[1,1,6,256,256]{4,3,2,1,0:T(8,128)(2,1)} %tiles_hbm.1, s32[1,1,6]{2,1,0:T(1,128)S(1)} %copy-done.1, s32[1,1,6]{2,1,0:T(1,128)S(1)} %copy-done.2, s32[1,1]{1,0:T(1,128)S(6)} %copy.7.counts_hbm), custom_call_target="tpu_custom_call" | custom-call | flops 16777216 | bytes 1048576 | tf_op jit(solution)/shard_map/pallas_call | solution.py:314
  47.4 0.6 %copy.8 = f32[4,4,256]{2,1,0:T(4,128)} copy(f32[4,4,256]{2,1,0:T(4,128)S(1)} %shard_map.55) | data formatting | bytes 32768
Async XLA Ops:
  0.0 0.7 %copy-start.2 = (s32[1,1,6]{2,1,0:T(1,128)S(1)}, s32[1,1,6]{2,1,0:T(1,128)}, u32[]{:S(2)}) copy-start(s32[1,1,6]{2,1,0:T(1,128)} %cols_hbm.1) | copy-start | bytes 76
  0.0 0.7 %copy-start.1 = (s32[1,1,6]{2,1,0:T(1,128)S(1)}, s32[1,1,6]{2,1,0:T(1,128)}, u32[]{:S(2)}) copy-start(s32[1,1,6]{2,1,0:T(1,128)} %rows_hbm.1) | copy-start | bytes 76
  0.7 0.7 %copy-start = (bf16[4,4,256]{2,1,0:T(4,128)(2,1)S(1)}, bf16[4,4,256]{2,1,0:T(4,128)(2,1)}, u32[]{:S(2)}) copy-start(bf16[4,4,256]{2,1,0:T(4,128)(2,1)} %vec_hbm.1) | copy-start | bytes 24580

commit v4 on v3

--- a/solution.py
+++ b/solution.py
@@ -17,9 +17,9 @@
 LANES = 128
 NONE = -(2**20)
 
-GROUPS = 13
-H_VEC, X_CODE, Y_CODE, Z_CODE, Z_VEC, X_VEC, Y_VEC = range(7)
-Y_PROD, Z_SUM, Z_PROD, Y_SUM, X_PROD, H_PROD = range(7, GROUPS)
+GROUPS = 15
+C_VEC, H_VEC, X_CODE, Y_CODE, Z_CODE, Z_VEC, X_NEAR, X_FAR, Y_VEC = range(9)
+Y_PROD, Z_SUM, Z_PROD, Y_SUM, X_PROD, H_PROD = range(9, GROUPS)
 
 
 def widen(row_of):
@@ -51,7 +51,7 @@
     vec_hbm, tiles_hbm, rows_hbm, cols_hbm, counts_hbm,
     out_ref,
     vin, tiles, rows_s, cols_s, counts_s,
-    vz, vw, vx, ccode, zcode, rcode, ysend, yrecv, yprod, zprod, rprod,
+    vz, vx, ccode, zcode, rcode, ysend, yrecv, yprod, zprod, rprod,
     zsend, zrecv, ssend, srecv, wsend, wrecv, y_place, z_place,
     local_sem, send_sem, recv_sem,
 ):
@@ -67,17 +67,20 @@
     def at(y_, z_, x_, w_):
         return (y_ * nz + z_, x_ * nw + w_)
 
-    def peers(me, n, place_of):
+    def peers(me, n, place_of, line=False):
         out = []
-        for k in sorted(range(1, n), key=lambda k: -min(k, n - k)):
+        for k in sorted(range(1, n), key=lambda k: min(k, n - k) * (1 if line else -1)):
             p = lax.rem(me + k, n)
             out.append((p, place_of(p)))
         return out
 
     y_peers = peers(y, ny, lambda p: at(p, z, x, w))
-    z_peers = peers(z, nz, lambda p: at(y, p, x, w))
+    z_peers = peers(z, nz, lambda p: at(y, p, x, w), line=True)
     x_peers = peers(x, nx, lambda p: at(y, z, p, w))
-    w_peers = peers(w, nw, lambda p: at(y, z, x, p))
+    cores = [h * nc + lax.rem(w + k, nc) for k in range(nc)]
+    core_peers = [(p, at(y, z, x, p)) for p in cores[1:]]
+    far_peers = [(p, at(y, z, x, p)) for p in [nw - nc - h * nc + (c - h * nc) for c in cores]]
+    w_peers = far_peers + core_peers
 
     locals_ = [
         pltpu.make_async_copy(src, dst, local_sem.at[i])
@@ -93,7 +96,8 @@
     ]
     locals_[0].start()
     barrier = pltpu.get_barrier_semaphore()
-    everyone = [device_id for _, device_id in w_peers + z_peers + y_peers + x_peers]
+    ordered = w_peers[:1] + y_peers[:3] + z_peers[:5] + w_peers[1:] + y_peers[3:] + x_peers + z_peers[5:]
+    everyone = [device_id for _, device_id in ordered]
     for device_id in everyone:
         pl.semaphore_signal(barrier, inc=1, device_id=device_id, device_id_type=MESH)
     for copy in locals_[1:]:
@@ -126,7 +130,7 @@
     own = jnp.concatenate([vin[j].astype(jnp.float32) for j in range(VB)], axis=0)
     own = own.astype(jnp.bfloat16)
     vz[z] = own
-    vw[w] = own
+    vx[x, w] = own
     for i in (1, 2, 3):
         locals_[i].wait()
     live = counts_s[0, 0]
@@ -169,18 +173,23 @@
 
     pl.semaphore_wait(barrier, len(everyone))
 
-    send_all(H_VEC, w_peers, lambda p: vw.at[w], vw.at[w])
+    send_all(H_VEC, far_peers, lambda p: vx.at[x, w], vx.at[x, w])
+    send_all(C_VEC, core_peers, lambda p: vx.at[x, w], vx.at[x, w])
     send_all(Z_VEC, z_peers, lambda p: vz.at[z], vz.at[z])
     send_all(Y_CODE, y_peers, lambda p: ccode.at[y], ccode.at[y])
     send_all(X_CODE, x_peers, lambda p: rcode.at[x], rcode.at[x])
 
     def slab_vectors():
-        wait(recv_sem.at[H_VEC], vw.at[pl.ds(0, nw - 1)])
-        vx[x] = vw[...].reshape(nw * ROWS, TILE)
-        send_all(X_VEC, x_peers, lambda p: vx.at[x], vx.at[x])
+        wait(recv_sem.at[C_VEC], vx.at[0, pl.ds(0, nc - 1)])
+        near = vx.at[x, pl.ds(h * nc, nc)]
+        send_all(X_NEAR, x_peers, lambda p: near, near)
+        wait(recv_sem.at[H_VEC], vx.at[0, pl.ds(0, nw - nc)])
+        far = vx.at[x, pl.ds((nh - 1 - h) * nc, nc)]
+        send_all(X_FAR, x_peers, lambda p: far, far)
 
     def column_products():
-        wait(recv_sem.at[X_VEC], vx.at[pl.ds(0, nx - 1)])
+        wait(recv_sem.at[X_NEAR], vx.at[pl.ds(0, nx - 1), pl.ds(0, nc)])
+        wait(recv_sem.at[X_FAR], vx.at[pl.ds(0, nx - 1), pl.ds(0, nw - nc)])
         row_vectors = jnp.dot(
             row_sel, vx[...].reshape(slab_rows, TILE), preferred_element_type=jnp.float32
         )
@@ -274,10 +283,19 @@
 
     pl.when(jnp.logical_not(columns_first))(column_sums)
 
-    wait(recv_sem.at[H_PROD], wrecv.at[pl.ds(0, nw - 1)])
-    total = wrecv[0]
-    for p in range(1, nw):
-        total = total + wrecv[p]
+    wait(send_sem.at[C_VEC], vx.at[0, pl.ds(0, nc - 1)])
+    wait(send_sem.at[H_VEC], vx.at[0, pl.ds(0, nw - nc)])
+    wait(send_sem.at[X_CODE], rcode.at[pl.ds(0, nx - 1)])
+    wait(send_sem.at[Y_CODE], ccode.at[pl.ds(0, ny - 1)])
+    wait(send_sem.at[Z_CODE], zcode.at[pl.ds(0, nz - 1)])
+    wait(send_sem.at[Z_VEC], vz.at[pl.ds(0, nz - 1)])
+    wait(send_sem.at[X_NEAR], vx.at[pl.ds(0, nx - 1), pl.ds(0, nc)])
+    wait(send_sem.at[X_FAR], vx.at[pl.ds(0, nx - 1), pl.ds(0, nw - nc)])
+    wait(send_sem.at[Y_VEC], ysend.at[pl.ds(0, ny - 1)])
+    wait(send_sem.at[Y_PROD], yprod.at[pl.ds(0, ny - 1), pl.ds(0, live_rows)])
+    wait(send_sem.at[Z_PROD], zprod.at[pl.ds(0, nz - 1), pl.ds(0, live_rows)])
+    wait(send_sem.at[X_PROD], rprod.at[pl.ds(0, nx - 1), pl.ds(0, live_rows)])
+
     wait(recv_sem.at[Y_SUM], srecv.at[pl.ds(0, ny - 1)])
     right = srecv[0]
     for p in range(1, ny):
@@ -286,23 +304,15 @@
     left = zrecv[0]
     for p in range(1, nz):
         left = left + zrecv[p]
-    total = total + jnp.concatenate([left, right], axis=1)
-    for j in range(VB):
-        out_ref[j] = total[NVEC * j : NVEC * (j + 1), :]
-
-    wait(send_sem.at[H_VEC], vw.at[pl.ds(0, nw - 1)])
-    wait(send_sem.at[X_CODE], rcode.at[pl.ds(0, nx - 1)])
-    wait(send_sem.at[Y_CODE], ccode.at[pl.ds(0, ny - 1)])
-    wait(send_sem.at[Z_VEC], vz.at[pl.ds(0, nz - 1)])
-    wait(send_sem.at[X_VEC], vx.at[pl.ds(0, nx - 1)])
-    wait(send_sem.at[Y_VEC], ysend.at[pl.ds(0, ny - 1)])
-    wait(send_sem.at[Z_CODE], zcode.at[pl.ds(0, nz - 1)])
-    wait(send_sem.at[Y_PROD], yprod.at[pl.ds(0, ny - 1), pl.ds(0, live_rows)])
-    wait(send_sem.at[Z_PROD], zprod.at[pl.ds(0, nz - 1), pl.ds(0, live_rows)])
-    wait(send_sem.at[X_PROD], rprod.at[pl.ds(0, nx - 1), pl.ds(0, live_rows)])
+    total = jnp.concatenate([left, right], axis=1)
     wait(send_sem.at[Z_SUM], zsend.at[pl.ds(0, nz - 1)])
     wait(send_sem.at[Y_SUM], ssend.at[pl.ds(0, ny - 1)])
     wait(send_sem.at[H_PROD], wsend.at[pl.ds(0, nw - 1)])
+    wait(recv_sem.at[H_PROD], wrecv.at[pl.ds(0, nw - 1)])
+    for p in range(nw):
+        total = total + wrecv[p]
+    for j in range(VB):
+        out_ref[j] = total[NVEC * j : NVEC * (j + 1), :]
 
 
 def on_device(sizes, vectors, tiles, tile_rows, tile_cols, tile_counts):
@@ -313,7 +323,7 @@
     vmem, smem = pltpu.VMEM, pltpu.SMEM
     return pl.pallas_call(
         functools.partial(kernel, sizes),
-        out_shape=jax.ShapeDtypeStruct(vectors.shape, f32),
+        out_shape=pltpu.VMEM(vectors.shape, f32),
         in_specs=[pl.BlockSpec(memory_space=pltpu.HBM)] * 5,
         out_specs=pl.BlockSpec(memory_space=pltpu.VMEM),
         scratch_shapes=[
@@ -323,8 +333,7 @@
             smem(tile_cols.shape, i32),
             smem(tile_counts.shape, i32),
             vmem((nz, ROWS, TILE), bf16),
-            vmem((nw, ROWS, TILE), bf16),
-            vmem((nx, nw * ROWS, TILE), bf16),
+            vmem((nx, nw, ROWS, TILE), bf16),
             vmem((ny, PAD, LANES), i32),
             vmem((nz, PAD, LANES), i32),
             vmem((nx, PAD, LANES), i32),
@@ -346,7 +355,7 @@
             pltpu.SemaphoreType.DMA((GROUPS,)),
         ],
         compiler_params=pltpu.CompilerParams(
-            collective_id=0, has_side_effects=True, vmem_limit_bytes=55000 * 2**10
+            collective_id=0, has_side_effects=True, vmem_limit_bytes=60 * 2**20
         ),
         cost_estimate=pl.CostEstimate(
             flops=2**24, bytes_accessed=2**20, transcendentals=0

time: 48.2 us -> 47.5 us (0.985)
  local copies, waits for them, and re-layouts: 1.31 us -> 0.61 us
    unnamed x7 -> x1, local copies, waits for them, and re-layouts: 1.31 us -> 0.61 us
where the time goes in v4:
time: 47.5 us; the launch traced here: 47.3 us
  Pallas kernels  46 us (97%)
  between operations  0.66 us (1%)
  local copies, waits for them, and re-layouts  0.61 us (1%)
    pallas_call x1, Pallas kernels, on_device(): pl.pallas_call(functools.partial(kernel, sizes), out_shape=pltpu.VMEM(vec...  46 us

profile of v4, /device:TPU:1, one launch (start us, length us, event | category | flops | bytes accessed | tf_op | source)
XLA Modules:
  0.0 47.3 jit_solution(15338927293635689337)
XLA Ops:
  0.7 46.0 %shard_map.55 = f32[4,4,256]{2,1,0:T(4,128)S(1)} custom-call(bf16[4,4,256]{2,1,0:T(4,128)(2,1)} %vec_hbm.1, bf16[1,1,6,256,256]{4,3,2,1,0:T(8,128)(2,1)} %tiles_hbm.1, s32[1,1,6]{2,1,0:T(1,128)} %rows_hbm.1, s32[1,1,6]{2,1,0:T(1,128)} %cols_hbm.1, s32[1,1]{1,0:T(1,128)S(6)} %copy.8.counts_hbm), custom_call_target="tpu_custom_call" | custom-call | flops 16777216 | bytes 1048576 | tf_op jit(solution)/shard_map/pallas_call | solution.py:324
  46.7 0.6 %copy.7 = f32[4,4,256]{2,1,0:T(4,128)} copy(f32[4,4,256]{2,1,0:T(4,128)S(1)} %shard_map.55) | data formatting | bytes 32768

commit v5 on v4

--- a/solution.py
+++ b/solution.py
@@ -17,9 +17,9 @@
 LANES = 128
 NONE = -(2**20)
 
-GROUPS = 15
-C_VEC, H_VEC, X_CODE, Y_CODE, Z_CODE, Z_VEC, X_NEAR, X_FAR, Y_VEC = range(9)
-Y_PROD, Z_SUM, Z_PROD, Y_SUM, X_PROD, H_PROD = range(9, GROUPS)
+GROUPS = 17
+C_VEC, H_VEC, D_VEC, X_CODE, Y_CODE, Z_CODE, Z_VEC, X_NEAR, X_FAR, X_DIAG, Y_VEC = range(11)
+Y_PROD, Z_SUM, Z_PROD, Y_SUM, X_PROD, H_PROD = range(11, GROUPS)
 
 
 def widen(row_of):
@@ -80,7 +80,7 @@
     cores = [h * nc + lax.rem(w + k, nc) for k in range(nc)]
     core_peers = [(p, at(y, z, x, p)) for p in cores[1:]]
     far_peers = [(p, at(y, z, x, p)) for p in [nw - nc - h * nc + (c - h * nc) for c in cores]]
-    w_peers = far_peers + core_peers
+    w_peers = far_peers[::-1] + core_peers
 
     locals_ = [
         pltpu.make_async_copy(src, dst, local_sem.at[i])
@@ -173,7 +173,8 @@
 
     pl.semaphore_wait(barrier, len(everyone))
 
-    send_all(H_VEC, far_peers, lambda p: vx.at[x, w], vx.at[x, w])
+    send_all(D_VEC, far_peers[1:], lambda p: vx.at[x, w], vx.at[x, w])
+    send_all(H_VEC, far_peers[:1], lambda p: vx.at[x, w], vx.at[x, w])
     send_all(C_VEC, core_peers, lambda p: vx.at[x, w], vx.at[x, w])
     send_all(Z_VEC, z_peers, lambda p: vz.at[z], vz.at[z])
     send_all(Y_CODE, y_peers, lambda p: ccode.at[y], ccode.at[y])
@@ -183,13 +184,15 @@
         wait(recv_sem.at[C_VEC], vx.at[0, pl.ds(0, nc - 1)])
         near = vx.at[x, pl.ds(h * nc, nc)]
         send_all(X_NEAR, x_peers, lambda p: near, near)
-        wait(recv_sem.at[H_VEC], vx.at[0, pl.ds(0, nw - nc)])
-        far = vx.at[x, pl.ds((nh - 1 - h) * nc, nc)]
-        send_all(X_FAR, x_peers, lambda p: far, far)
+        for arrived, onward, (p, _) in zip((H_VEC, D_VEC), (X_FAR, X_DIAG), far_peers):
+            wait(recv_sem.at[arrived], vx.at[0, 0])
+            far = vx.at[x, p]
+            send_all(onward, x_peers, lambda p: far, far)
 
     def column_products():
         wait(recv_sem.at[X_NEAR], vx.at[pl.ds(0, nx - 1), pl.ds(0, nc)])
-        wait(recv_sem.at[X_FAR], vx.at[pl.ds(0, nx - 1), pl.ds(0, nw - nc)])
+        wait(recv_sem.at[X_FAR], vx.at[pl.ds(0, nx - 1), 0])
+        wait(recv_sem.at[X_DIAG], vx.at[pl.ds(0, nx - 1), 0])
         row_vectors = jnp.dot(
             row_sel, vx[...].reshape(slab_rows, TILE), preferred_element_type=jnp.float32
         )
@@ -284,13 +287,15 @@
     pl.when(jnp.logical_not(columns_first))(column_sums)
 
     wait(send_sem.at[C_VEC], vx.at[0, pl.ds(0, nc - 1)])
-    wait(send_sem.at[H_VEC], vx.at[0, pl.ds(0, nw - nc)])
+    wait(send_sem.at[H_VEC], vx.at[0, 0])
+    wait(send_sem.at[D_VEC], vx.at[0, 0])
     wait(send_sem.at[X_CODE], rcode.at[pl.ds(0, nx - 1)])
     wait(send_sem.at[Y_CODE], ccode.at[pl.ds(0, ny - 1)])
     wait(send_sem.at[Z_CODE], zcode.at[pl.ds(0, nz - 1)])
     wait(send_sem.at[Z_VEC], vz.at[pl.ds(0, nz - 1)])
     wait(send_sem.at[X_NEAR], vx.at[pl.ds(0, nx - 1), pl.ds(0, nc)])
-    wait(send_sem.at[X_FAR], vx.at[pl.ds(0, nx - 1), pl.ds(0, nw - nc)])
+    wait(send_sem.at[X_FAR], vx.at[pl.ds(0, nx - 1), 0])
+    wait(send_sem.at[X_DIAG], vx.at[pl.ds(0, nx - 1), 0])
     wait(send_sem.at[Y_VEC], ysend.at[pl.ds(0, ny - 1)])
     wait(send_sem.at[Y_PROD], yprod.at[pl.ds(0, ny - 1), pl.ds(0, live_rows)])
     wait(send_sem.at[Z_PROD], zprod.at[pl.ds(0, nz - 1), pl.ds(0, live_rows)])

time: 47.5 us -> 47.2 us (level)
  no operation moved by 1% of the time
where the time goes in v5:
time: 47.2 us; the launch traced here: 47 us
  Pallas kernels  45.8 us (97%)
  between operations  0.66 us (1%)
  local copies, waits for them, and re-layouts  0.61 us (1%)
    pallas_call x1, Pallas kernels, on_device(): pl.pallas_call(functools.partial(kernel, sizes), out_shape=pltpu.VMEM(vec...  45.8 us

profile of v5, /device:TPU:1, one launch (start us, length us, event | category | flops | bytes accessed | tf_op | source)
XLA Modules:
  0.0 47.0 jit_solution(10324719369313095120)
XLA Ops:
  0.7 45.8 %shard_map.55 = f32[4,4,256]{2,1,0:T(4,128)S(1)} custom-call(bf16[4,4,256]{2,1,0:T(4,128)(2,1)} %vec_hbm.1, bf16[1,1,6,256,256]{4,3,2,1,0:T(8,128)(2,1)} %tiles_hbm.1, s32[1,1,6]{2,1,0:T(1,128)} %rows_hbm.1, s32[1,1,6]{2,1,0:T(1,128)} %cols_hbm.1, s32[1,1]{1,0:T(1,128)S(6)} %copy.8.counts_hbm), custom_call_target="tpu_custom_call" | custom-call | flops 16777216 | bytes 1048576 | tf_op jit(solution)/shard_map/pallas_call | solution.py:329
  46.4 0.6 %copy.7 = f32[4,4,256]{2,1,0:T(4,128)} copy(f32[4,4,256]{2,1,0:T(4,128)S(1)} %shard_map.55) | data formatting | bytes 32768
